TPU v7x, 32 devices: a whole 2x2x4 slice. The times are simulated.
32 devices in a mesh: groups: 2 (over y), seq: 4 (over z), tile: 2 (over x), chan: 2 (over core).
Axes of the slice: x: 2, y: 2, z: 4, core: 2. Of those that a mesh axis runs over, the one named last changes fastest.
Arguments:
- latents: bfloat16 [2, 7680, 384], P('tile', ('groups', 'seq'), 'chan'), parts along dimension 1, may hold values from -6 to 6
- norm_gain: float32 [384], replicated, may hold values from 0.1 to 1.9
- conv_weight: bfloat16 [3, 3, 3, 384, 384], P(None, None, None, None, 'chan'), may hold values from -0.0625 to 0.0625
- conv_bias: float32 [384], P('chan'), may hold values from -3 to 3
- upsample_weight: bfloat16 [3, 3, 384, 192], P(None, None, None, 'chan'), may hold values from -0.109375 to 0.109375
- upsample_bias: float32 [192], P('chan'), may hold values from -3 to 3
Outputs:
- decoded: bfloat16 [8, 192, 20, 384], P(None, ('groups', 'tile'), 'seq', 'chan'), parts along dimension 1
There are 2 independent parts, one for each index of `groups`. A program takes and returns all parts, laid end to end along the dimension named above; an argument that names none is the same for every part. Nothing has to cross between parts.
All inputs are finite; a program needn't handle non-finite values.
Results may differ from a plain program's by a relative error of at most 0.005.
Values may be sent and summed in bfloat16 or wider, within the bound.
A program may use at most 64 MiB of HBM per device.

v0:
```python
import jax
import jax.numpy as jnp
from jax import lax
from jax.sharding import PartitionSpec as P

FRAMES = 8
ROWS_DEV = 24
COLS_DEV = 5


norm_eps = 1e-06


def extended(cells, sides, width):
    for axis, dim in sides:
        count = lax.axis_size(axis)
        ends = count - 1
        head = lax.slice_in_dim(cells, 0, width, axis=dim)
        tail = lax.slice_in_dim(cells, cells.shape[dim] - width, cells.shape[dim], axis=dim)
        cells = jnp.concatenate(
            [
                lax.ppermute(tail, axis, [(i, (i + 1) % count) for i in range(ends)]),
                cells,
                lax.ppermute(head, axis, [((i + 1) % count, i) for i in range(ends)]),
            ],
            axis=dim,
        )
    return cells


def activate(padded, norm_gain):
    values = padded.astype(jnp.float32)
    scale = lax.rsqrt(jnp.mean(values * values, axis=-1, keepdims=True) + norm_eps)
    return jax.nn.silu(values * scale * norm_gain).astype(jnp.bfloat16)


def body(latents, norm_gain, conv_weight, conv_bias, upsample_weight, upsample_bias):
    seq_count = lax.axis_size("seq")
    local_chan = conv_bias.shape[0]
    rows_src = FRAMES * ROWS_DEV // seq_count
    whole = lax.all_gather(latents[0], "chan", axis=1, tiled=True)
    arranged = whole.reshape(rows_src, seq_count, COLS_DEV, whole.shape[1])
    regrouped = lax.all_to_all(arranged, "seq", split_axis=1, concat_axis=0, tiled=True)
    full_field = regrouped.reshape(FRAMES, ROWS_DEV, COLS_DEV, whole.shape[1])
    padded = extended(full_field, (("seq", 2), ("tile", 1)), 1)
    field_own = lax.dynamic_slice_in_dim(
        full_field, lax.axis_index("chan") * local_chan, local_chan, 3
    )
    activation = activate(padded, norm_gain)
    shifted = jnp.pad(activation, ((2, 0), (0, 0), (0, 0), (0, 0)))
    conv_out = lax.conv_general_dilated(
        shifted[None],
        conv_weight,
        (1, 1, 1),
        "VALID",
        dimension_numbers=("NDHWC", "DHWIO", "NDHWC"),
        preferred_element_type=jnp.float32,
    )[0]
    middle = (field_own.astype(jnp.float32) + conv_out + conv_bias).astype(jnp.bfloat16)
    middle_rim = extended(middle, (("seq", 2), ("tile", 1)), 1)
    middle_full = lax.all_gather(middle_rim, "chan", axis=3, tiled=True)
    upsampled = jnp.repeat(jnp.repeat(middle_full, 2, axis=1), 2, axis=2)[:, 1:-1, 1:-1, :]
    image = lax.conv_general_dilated(
        upsampled,
        upsample_weight,
        (1, 1),
        "VALID",
        dimension_numbers=("NHWC", "HWIO", "NHWC"),
        preferred_element_type=jnp.float32,
    )
    image = image + upsample_bias
    out_chan = upsample_bias.shape[0]
    image = image.reshape(FRAMES, 2 * ROWS_DEV, COLS_DEV, 2, out_chan)
    image = jnp.transpose(image, (0, 1, 2, 4, 3)).reshape(
        FRAMES, 2 * ROWS_DEV, COLS_DEV, 2 * out_chan
    )
    return image.astype(jnp.bfloat16)


def solution(mesh):
    in_specs = (
        P("tile", ("groups", "seq"), "chan"),
        P(),
        P(None, None, None, None, "chan"),
        P("chan"),
        P(None, None, None, "chan"),
        P("chan"),
    )
    out_specs = P(None, ("groups", "tile"), "seq", "chan")
    return jax.shard_map(body, mesh=mesh, in_specs=in_specs, out_specs=out_specs, check_vma=False)
```

profile of v0, /device:TPU:0, one launch (start us, length us, event | category | flops | bytes accessed | tf_op | source)
XLA Modules:
  0.0 154.0 jit_solution(12144148786594133457)
XLA Ops:
  6.5 2.8 %all-gather = bf16[1,960,384]{1,2,0:T(8,128)(2,1)S(1)} all-gather(bf16[1,960,192]{1,2,0:T(8,128)(2,1)} %param.6), channel_id=2, replica_groups=mesh['groups'=2,'seq'=4,'tile'=2,'chan'=2] {'chan'}, dimensions={2}, use_global_device_ids=true | all-gather | bytes 1105920 | tf_op jit(solution)/shard_map/all_gather | solution.py:41
  10.3 25.4 %all_to_all.15 = bf16[48,4,5,384]{3,0,2,1:T(8,128)(2,1)S(1)} all-to-all(bf16[48,4,5,384]{3,0,2,1:T(8,128)(2,1)S(1)} %copy.27), channel_id=1, replica_groups=mesh['groups'=2,'seq'=4,'tile'=2,'chan'=2] {'seq'}, dimensions={1} | all-to-all | bytes 1474560 | tf_op jit(solution)/shard_map/all_to_all | solution.py:43
  35.8 2.3 %collective-permute-start = (bf16[8,24,1,384]{3,1,0,2:T(8,128)(2,1)S(1)}, bf16[8,24,1,384]{3,1,0,2:T(8,128)(2,1)S(1)}, u32[]{:S(2)}, u32[]{:S(2)}) collective-permute-start(bf16[8,24,1,384]{3,1,0,2:T(8,128)(2,1)S(1)} %get-tuple-element.7), channel_id=1, source_target_pairs={{0,4},{4,8},{8,12},{1,5},{5,9},{9,13},{2,6},{6,10},{10,14},{3,7},{... | collective-permute-start | bytes 442376 | tf_op jit(solution)/shard_map/ppermute | solution.py:22
  38.1 1.3 collective-permute-start.1
  39.4 1.3 collective-permute-done
  40.7 4.4 %collective-permute-done.1 = bf16[8,24,1,384]{3,1,0,2:T(8,128)(2,1)S(1)} collective-permute-done((bf16[8,24,1,384]{3,1,0,2:T(8,128)(2,1)S(1)}, bf16[8,24,1,384]{3,1,0,2:T(8,128)(2,1)S(1)}, u32[]{:S(2)}, u32[]{:S(2)}) %collective-permute-start.1) | collective-permute-done | bytes 147488 | tf_op jit(solution)/shard_map/ppermute | solution.py:24
  45.2 3.4 %collective-permute-start.2 = (bf16[8,1,7,384]{3,1,0,2:T(2,128)(2,1)S(1)}, bf16[8,1,7,384]{3,1,0,2:T(2,128)(2,1)S(1)}, u32[]{:S(2)}, u32[]{:S(2)}) collective-permute-start(bf16[8,1,7,384]{3,1,0,2:T(2,128)(2,1)S(1)} %get-tuple-element.5), channel_id=1, source_target_pairs={{0,2},{1,3},{4,6},{5,7},{8,10},{9,11},{12,14},{13,15},{16,18},{17,... | collective-permute-start | bytes 129032 | tf_op jit(solution)/shard_map/ppermute | solution.py:22
  48.7 1.3 collective-permute-start.3
  50.7 4.3 %collective-permute-done.3 = bf16[8,1,7,384]{3,1,0,2:T(2,128)(2,1)S(1)} collective-permute-done((bf16[8,1,7,384]{3,1,0,2:T(2,128)(2,1)S(1)}, bf16[8,1,7,384]{3,1,0,2:T(2,128)(2,1)S(1)}, u32[]{:S(2)}, u32[]{:S(2)}) %collective-permute-start.3) | collective-permute-done | bytes 43040 | tf_op jit(solution)/shard_map/ppermute | solution.py:24
  55.8 1.5 fusion.9
  57.9 29.8 %fusion = f32[1,8,24,5,192]{4,0,3,2,1:T(1,128)S(1)} fusion(bf16[3,3,3,384,192]{3,4,2,1,0:T(8,128)(2,1)S(1)} %copy-done.3, bf16[1,10,26,7,384]{4,2,1,3,0:T(8,128)(2,1)S(1)} %pad_bitcast_fusion), kind=kOutput, calls=%fused_computation.2 | convolution fusion | flops 3822059520 | bytes 6116352 | tf_op jit(solution)/shard_map/conv_general_dilated | solution.py:51
  88.0 2.5 %collective-permute-start.4 = (bf16[8,24,1,192]{3,1,0,2:T(8,128)(2,1)S(1)}, bf16[8,24,1,192]{3,1,0,2:T(8,128)(2,1)S(1)}, u32[]{:S(2)}, u32[]{:S(2)}) collective-permute-start(bf16[8,24,1,192]{3,1,0,2:T(8,128)(2,1)S(1)} %get-tuple-element.11), channel_id=1, source_target_pairs={{0,4},{4,8},{8,12},{1,5},{5,9},{9,13},{2,6},{6,10},{10,14},{3,7},{... | collective-permute-start | bytes 221192 | tf_op jit(solution)/shard_map/ppermute | solution.py:22
  90.5 1.3 collective-permute-start.5
  91.8 0.9 collective-permute-done.4
  92.7 4.3 %collective-permute-done.5 = bf16[8,24,1,192]{3,1,0,2:T(8,128)(2,1)S(1)} collective-permute-done((bf16[8,24,1,192]{3,1,0,2:T(8,128)(2,1)S(1)}, bf16[8,24,1,192]{3,1,0,2:T(8,128)(2,1)S(1)}, u32[]{:S(2)}, u32[]{:S(2)}) %collective-permute-start.5) | collective-permute-done | bytes 73760 | tf_op jit(solution)/shard_map/ppermute | solution.py:24
  97.1 1.5 %collective-permute-start.6 = (bf16[8,1,7,192]{3,1,0,2:T(2,128)(2,1)S(1)}, bf16[8,1,7,192]{3,1,0,2:T(2,128)(2,1)S(1)}, u32[]{:S(2)}, u32[]{:S(2)}) collective-permute-start(bf16[8,1,7,192]{3,1,0,2:T(2,128)(2,1)S(1)} %get-tuple-element.9), channel_id=1, source_target_pairs={{0,2},{1,3},{4,6},{5,7},{8,10},{9,11},{12,14},{13,15},{16,18},{17,... | collective-permute-start | bytes 64520 | tf_op jit(solution)/shard_map/ppermute | solution.py:22
  98.7 1.3 collective-permute-start.7
  100.5 4.3 %collective-permute-done.7 = bf16[8,1,7,192]{3,1,0,2:T(2,128)(2,1)S(1)} collective-permute-done((bf16[8,1,7,192]{3,1,0,2:T(2,128)(2,1)S(1)}, bf16[8,1,7,192]{3,1,0,2:T(2,128)(2,1)S(1)}, u32[]{:S(2)}, u32[]{:S(2)}) %collective-permute-start.7) | collective-permute-done | bytes 21536 | tf_op jit(solution)/shard_map/ppermute | solution.py:24
  105.3 3.5 %copy.33 = bf16[8,26,7,192]{1,0,2,3:T(8,128)(2,1)} copy(bf16[8,26,7,192]{3,1,0,2:T(8,128)(2,1)S(1)} %pad_maximum_fusion.1) | data formatting | bytes 1118208 | tf_op jit(solution)/shard_map/concatenate | solution.py:20
  108.8 14.2 %all-gather.3.cloned.1.call-done = bf16[8,26,7,384]{1,0,2,3:T(8,128)(2,1)} async-done(((bf16[8,26,7,192]{1,0,2,3:T(8,128)(2,1)}), bf16[8,26,7,384]{1,0,2,3:T(8,128)(2,1)}) %all-gather.3.cloned.1.call-update) | async-done | bytes 1118224 | tf_op jit(solution)/shard_map/all_gather | solution.py:61
  122.9 9.9 %copy.34 = bf16[8,26,7,384]{3,0,2,1:T(8,128)(2,1)S(1)} copy(bf16[8,26,7,384]{1,0,2,3:T(8,128)(2,1)} %all-gather.3.cloned.1.call-done) | data formatting | bytes 2236416 | tf_op jit(solution)/shard_map/all_gather | solution.py:61
  133.7 8.0 %add_convert_fusion = bf16[8,48,10,96]{3,0,2,1:T(8,128)(2,1)} fusion(bf16[8,52,14,384]{3,0,2,1:T(8,128)(2,1)S(1)} %bitcast.30, bf16[3,3,384,96]{2,3,1,0:T(8,128)(2,1)S(1)} %copy-done, f32[96]{0:T(128)S(1)} %copy-done.4), kind=kOutput, calls=%fused_computation.12 | convolution fusion | flops 2548776960 | bytes 5874048 | tf_op jit(solution)/shard_map/conv_general_dilated | solution.py:63
  141.7 2.6 %copy.35 = bf16[8,48,5,2,96]{1,0,3,4,2:T(8,128)(2,1)S(1)} copy(bf16[8,48,5,2,96]{4,0,3,2,1:T(8,128)(2,1)} %bitcast.31) | data formatting | bytes 1474560 | tf_op jit(solution)/shard_map/convert_element_type | solution.py:77
  144.4 2.8 %copy.36 = bf16[8,48,5,192]{3,1,2,0:T(8,128)(2,1)} copy(bf16[8,48,5,192]{1,0,3,2:T(8,128)(2,1)S(1)} %bitcast.29) | data formatting | bytes 1474560 | tf_op jit(solution)/shard_map/convert_element_type | solution.py:77
  (29 shorter events, 5.6 us)
Async XLA Ops:
  6.5 126.9 %copy-start = (bf16[3,3,384,96]{2,3,1,0:T(8,128)(2,1)S(1)}, bf16[3,3,384,96]{2,3,1,0:T(8,128)(2,1)}, u32[]{:S(2)}) copy-start(bf16[3,3,384,96]{2,3,1,0:T(8,128)(2,1)} %param.10) | copy-start | bytes 1990660
  6.5 116.4 %all-gather.3.cloned.1.call-start = ((), (), s32[]{:S(2)}) async-start(), calls=%async_computation.1 | async-start | bytes 8257536 | tf_op jit(solution)/shard_map/all_gather | solution.py:61
  10.3 45.5 %copy-start.1 = (f32[384]{0:T(512)S(1)}, f32[384]{0:T(512)}, u32[]{:S(2)}) copy-start(f32[384]{0:T(512)} %param.7) | copy-start | bytes 4612
  35.8 4.9 %collective-permute-start = (bf16[8,24,1,384]{3,1,0,2:T(8,128)(2,1)S(1)}, bf16[8,24,1,384]{3,1,0,2:T(8,128)(2,1)S(1)}, u32[]{:S(2)}, u32[]{:S(2)}) collective-permute-start(bf16[8,24,1,384]{3,1,0,2:T(8,128)(2,1)S(1)} %get-tuple-element.7), channel_id=1, source_target_pairs={{0,4},{4,8},{8,12},{1,5},{5,9},{9,13},{2,6},{6,10},{10,14},{3,7},{... | collective-permute-start | bytes 442376 | tf_op jit(solution)/shard_map/ppermute | solution.py:22
  38.1 7.0 %collective-permute-start.1 = (bf16[8,24,1,384]{3,1,0,2:T(8,128)(2,1)S(1)}, bf16[8,24,1,384]{3,1,0,2:T(8,128)(2,1)S(1)}, u32[]{:S(2)}, u32[]{:S(2)}) collective-permute-start(bf16[8,24,1,384]{3,1,0,2:T(8,128)(2,1)S(1)} %get-tuple-element.8), channel_id=1, source_target_pairs={{4,0},{8,4},{12,8},{5,1},{9,5},{13,9},{6,2},{10,6},{14,10},{7,3},{... | collective-permute-start | bytes 442376 | tf_op jit(solution)/shard_map/ppermute | solution.py:24
  45.2 5.5 %collective-permute-start.2 = (bf16[8,1,7,384]{3,1,0,2:T(2,128)(2,1)S(1)}, bf16[8,1,7,384]{3,1,0,2:T(2,128)(2,1)S(1)}, u32[]{:S(2)}, u32[]{:S(2)}) collective-permute-start(bf16[8,1,7,384]{3,1,0,2:T(2,128)(2,1)S(1)} %get-tuple-element.5), channel_id=1, source_target_pairs={{0,2},{1,3},{4,6},{5,7},{8,10},{9,11},{12,14},{13,15},{16,18},{17,... | collective-permute-start | bytes 129032 | tf_op jit(solution)/shard_map/ppermute | solution.py:22
  48.7 6.4 %collective-permute-start.3 = (bf16[8,1,7,384]{3,1,0,2:T(2,128)(2,1)S(1)}, bf16[8,1,7,384]{3,1,0,2:T(2,128)(2,1)S(1)}, u32[]{:S(2)}, u32[]{:S(2)}) collective-permute-start(bf16[8,1,7,384]{3,1,0,2:T(2,128)(2,1)S(1)} %get-tuple-element.6), channel_id=1, source_target_pairs={{2,0},{3,1},{6,4},{7,5},{10,8},{11,9},{14,12},{15,13},{18,16},{19,... | collective-permute-start | bytes 129032 | tf_op jit(solution)/shard_map/ppermute | solution.py:24
  55.8 2.1 %copy-start.3 = (bf16[3,3,3,384,192]{3,4,2,1,0:T(8,128)(2,1)S(1)}, bf16[3,3,3,384,192]{3,4,2,1,0:T(8,128)(2,1)}, u32[]{:S(2)}) copy-start(bf16[3,3,3,384,192]{3,4,2,1,0:T(8,128)(2,1)} %param.8) | copy-start | bytes 11943940
  57.9 29.8 %copy-start.2 = (f32[192]{0:T(256)S(1)}, f32[192]{0:T(256)}, u32[]{:S(2)}) copy-start(f32[192]{0:T(256)} %param.9) | copy-start | bytes 2308
  88.0 4.7 %collective-permute-start.4 = (bf16[8,24,1,192]{3,1,0,2:T(8,128)(2,1)S(1)}, bf16[8,24,1,192]{3,1,0,2:T(8,128)(2,1)S(1)}, u32[]{:S(2)}, u32[]{:S(2)}) collective-permute-start(bf16[8,24,1,192]{3,1,0,2:T(8,128)(2,1)S(1)} %get-tuple-element.11), channel_id=1, source_target_pairs={{0,4},{4,8},{8,12},{1,5},{5,9},{9,13},{2,6},{6,10},{10,14},{3,7},{... | collective-permute-start | bytes 221192 | tf_op jit(solution)/shard_map/ppermute | solution.py:22
  90.5 6.5 %collective-permute-start.5 = (bf16[8,24,1,192]{3,1,0,2:T(8,128)(2,1)S(1)}, bf16[8,24,1,192]{3,1,0,2:T(8,128)(2,1)S(1)}, u32[]{:S(2)}, u32[]{:S(2)}) collective-permute-start(bf16[8,24,1,192]{3,1,0,2:T(8,128)(2,1)S(1)} %get-tuple-element.12), channel_id=1, source_target_pairs={{4,0},{8,4},{12,8},{5,1},{9,5},{13,9},{6,2},{10,6},{14,10},{7,3},{... | collective-permute-start | bytes 221192 | tf_op jit(solution)/shard_map/ppermute | solution.py:24
  97.1 3.4 %collective-permute-start.6 = (bf16[8,1,7,192]{3,1,0,2:T(2,128)(2,1)S(1)}, bf16[8,1,7,192]{3,1,0,2:T(2,128)(2,1)S(1)}, u32[]{:S(2)}, u32[]{:S(2)}) collective-permute-start(bf16[8,1,7,192]{3,1,0,2:T(2,128)(2,1)S(1)} %get-tuple-element.9), channel_id=1, source_target_pairs={{0,2},{1,3},{4,6},{5,7},{8,10},{9,11},{12,14},{13,15},{16,18},{17,... | collective-permute-start | bytes 64520 | tf_op jit(solution)/shard_map/ppermute | solution.py:22
  98.7 6.1 %collective-permute-start.7 = (bf16[8,1,7,192]{3,1,0,2:T(2,128)(2,1)S(1)}, bf16[8,1,7,192]{3,1,0,2:T(2,128)(2,1)S(1)}, u32[]{:S(2)}, u32[]{:S(2)}) collective-permute-start(bf16[8,1,7,192]{3,1,0,2:T(2,128)(2,1)S(1)} %get-tuple-element.10), channel_id=1, source_target_pairs={{2,0},{3,1},{6,4},{7,5},{10,8},{11,9},{14,12},{15,13},{18,16},{19,... | collective-permute-start | bytes 64520 | tf_op jit(solution)/shard_map/ppermute | solution.py:24
  133.0 0.7 copy-start.4
Sparse Core Ops, SparseCore 0:
  108.9 13.9 all-gather.2
where the time goes:
time: 154 us
  matrix products  37.8 us (25%)
  waiting for transfers between devices  35 us (23%)
  blocking collectives  28.2 us (18%)
  local copies, waits for them, and re-layouts  21.3 us (14%)
  starting transfers between devices  14.8 us (10%)
  between operations  13.6 us (9%)
  other arithmetic  3.28 us (2%)
    conv_general_dilated x1, matrix products, body(): lax.conv_general_dilated(shifted[None], conv_weight, (1, 1, 1), 'VALID',...  29.8 us
    all_to_all x1, blocking collectives, body(): lax.all_to_all(arranged, 'seq', split_axis=1, concat_axis=0, tiled=True)  25.4 us
    ppermute x4, waiting for transfers between devices, extended(): lax.ppermute(head, axis, [((i + 1) % count, i) for i in range(ends)])  17.3 us
    all_gather x1, waiting for transfers between devices, body(): middle_full = lax.all_gather(middle_rim, 'chan', axis=3, tiled=True)  14.2 us
    all_gather x1, local copies, waits for them, and re-layouts, body(): middle_full = lax.all_gather(middle_rim, 'chan', axis=3, tiled=True)  9.9 us
    ppermute x4, starting transfers between devices, extended(): lax.ppermute(tail, axis, [(i, (i + 1) % count) for i in range(ends)])  9.67 us
    conv_general_dilated x1, matrix products, body(): lax.conv_general_dilated(upsampled, upsample_weight, (1, 1), 'VALID', dim...  8.02 us
    convert_element_type x2, local copies, waits for them, and re-layouts, body(): return image.astype(jnp.bfloat16)  5.44 us
  transfers between devices with their start and end apart: 9, of which 9 were waited for; matrix products, arithmetic and copies ran while one was open for 0% of the time, Pallas kernels for 0%

commit v1 on v0

--- a/solution.py
+++ b/solution.py
@@ -1,11 +1,17 @@
+import functools
+
 import jax
 import jax.numpy as jnp
 from jax import lax
+from jax.experimental import pallas as pl
+from jax.experimental.pallas import tpu as pltpu
 from jax.sharding import PartitionSpec as P
 
 FRAMES = 8
 ROWS_DEV = 24
 COLS_DEV = 5
+PITCH = 32
+MESH = pl.DeviceIdType.MESH
 
 
 norm_eps = 1e-06
@@ -34,7 +40,7 @@
     return jax.nn.silu(values * scale * norm_gain).astype(jnp.bfloat16)
 
 
-def body(latents, norm_gain, conv_weight, conv_bias, upsample_weight, upsample_bias):
+def plain_body(latents, norm_gain, conv_weight, conv_bias, upsample_weight, upsample_bias):
     seq_count = lax.axis_size("seq")
     local_chan = conv_bias.shape[0]
     rows_src = FRAMES * ROWS_DEV // seq_count
@@ -77,7 +83,327 @@
     return image.astype(jnp.bfloat16)
 
 
+def kernel(S, T, main_ref, tops_ref, bots_ref, gain_ref, cw_ref, cb_ref, uw_ref, ub_ref, out_ref,
+           recv, halo, act3, res, wv, wf, mid, up,
+           w_sem, a_send, a_recv, f_send, f_recv, h_send, h_recv, g_send, g_recv, m_send, m_recv, e_send, e_recv):
+    s, t, c = lax.axis_index("seq"), lax.axis_index("tile"), lax.axis_index("chan")
+    other = 1 - c
+    wide = COLS_DEV + 2
+    nf = FRAMES // S
+    half = main_ref.shape[2]
+    full = 2 * half
+
+    def weight_copy(dt, dh, dw):
+        return pltpu.make_async_copy(
+            cw_ref.at[dt, dh, dw],
+            wv.at[dt * 3 + dw, pl.ds(dh * full, full)],
+            w_sem.at[dt, dh, dw],
+        )
+
+    taps = [(dt, dh, dw) for dt in range(3) for dh in range(3) for dw in range(3)]
+    for tap in taps:
+        weight_copy(*tap).start()
+
+    barrier = pltpu.get_barrier_semaphore()
+    size = S * T * 2
+    me = (s * T + t) * 2 + c
+    for k in range(1, size):
+        peer = (me + k) % size
+        pl.semaphore_signal(
+            barrier, inc=1, device_id={"seq": peer // (2 * T), "tile": peer // 2 % T, "chan": peer % 2},
+            device_id_type=MESH,
+        )
+    pl.semaphore_wait(barrier, size - 1)
+
+    def remote(src, dst, send, recv_, **where):
+        return pltpu.make_async_remote_copy(
+            src_ref=src, dst_ref=dst, send_sem=send, recv_sem=recv_, device_id=where, device_id_type=MESH
+        )
+
+    def main_copy(k):
+        d = (s + S - k) % S
+        return remote(main_ref.at[pl.ds(d * COLS_DEV, wide)], recv.at[c, s], a_send.at[k], a_recv.at[k],
+                      seq=d, tile=t, chan=c)
+
+    def main_arrival(k):
+        q = (s + k) % S
+        return remote(main_ref.at[pl.ds(0, wide)], recv.at[c, q], a_send.at[k], a_recv.at[k], seq=q, tile=t, chan=c)
+
+    own_copy = pltpu.make_async_copy(main_ref.at[pl.ds(s * COLS_DEV, wide)], recv.at[c, s], a_recv.at[0])
+
+    def pass_on(k):
+        q = (s + k) % S
+        return remote(recv.at[c, q], recv.at[c, q], f_send.at[k], f_recv.at[k], seq=s, tile=t, chan=other)
+
+    def passed(k):
+        q = (s + k) % S
+        return remote(recv.at[other, q], recv.at[other, q], f_send.at[k], f_recv.at[k], seq=s, tile=t, chan=other)
+
+    def halo_copy(side, k):
+        d = (s + S - k) % S
+        src = tops_ref if side == 0 else bots_ref
+        to = t + 1 if side == 0 else t - 1
+        return remote(src.at[d], halo.at[c, side, s], h_send.at[side, k], h_recv.at[side, k], seq=d, tile=to, chan=c)
+
+    def halo_arrival(side, k):
+        q = (s + k) % S
+        return remote(tops_ref.at[0], halo.at[c, side, q], h_send.at[side, k], h_recv.at[side, k],
+                      seq=q, tile=t, chan=other)
+
+    def halo_on(side, k):
+        q = (s + k) % S
+        return remote(halo.at[c, side, q], halo.at[c, side, q], g_send.at[side, k], g_recv.at[side, k],
+                      seq=s, tile=t, chan=other)
+
+    def halo_passed(side, k):
+        q = (s + k) % S
+        return remote(halo.at[other, side, q], halo.at[other, side, q], g_send.at[side, k], g_recv.at[side, k],
+                      seq=s, tile=t, chan=other)
+
+    sends_halo = (t < T - 1, t > 0)
+    gets_halo = (t > 0, t < T - 1)
+
+    own_copy.start()
+    for k in range(S - 1, 0, -1):
+        main_copy(k).start()
+    for side in range(2):
+        @pl.when(sends_halo[side])
+        def _():
+            for k in range(S):
+                halo_copy(side, k).start()
+
+        @pl.when(jnp.logical_not(gets_halo[side]))
+        def _():
+            halo[:, side] = jnp.zeros(halo.shape[:1] + halo.shape[2:], halo.dtype)
+
+    @pl.when(s == 0)
+    def _():
+        mid[:, 0] = jnp.zeros(mid.shape[:1] + mid.shape[2:], mid.dtype)
+
+    @pl.when(s == S - 1)
+    def _():
+        mid[:, wide - 1] = jnp.zeros(mid.shape[:1] + mid.shape[2:], mid.dtype)
+
+    act3[:, 0:2] = jnp.zeros((wide, 2) + act3.shape[2:], act3.dtype)
+
+    out_half = uw_ref.shape[3]
+    source = lax.broadcasted_iota(jnp.int32, (out_half, 2 * out_half), 0)
+    target = lax.broadcasted_iota(jnp.int32, (out_half, 2 * out_half), 1)
+    spread = [jnp.where(target == 2 * source + j, 1.0, 0.0).astype(jnp.bfloat16) for j in range(2)]
+    row_taps = (((0,), (1, 2)), ((0, 1), (2,)))
+    col_taps = (((0,), ()), ((1, 2), (0, 1)), ((), (2,)))
+    for i in range(2):
+        for b in range(3):
+            for a in range(2):
+                total = None
+                for j in range(2):
+                    if not col_taps[b][j]:
+                        continue
+                    terms = [uw_ref[dr, dc].astype(jnp.float32) for dr in row_taps[i][a] for dc in col_taps[b][j]]
+                    value = functools.reduce(lambda u, v: u + v, terms).astype(jnp.bfloat16)
+                    part = jnp.dot(value, spread[j], preferred_element_type=jnp.float32)
+                    total = part if total is None else total + part
+                wf[i, b, a * full:(a + 1) * full] = total.astype(jnp.bfloat16)
+
+    gain = gain_ref[...]
+
+    @pl.loop(0, S)
+    def _(k):
+        q = (s + k) % S
+
+        @pl.when(k == 0)
+        def _():
+            own_copy.wait()
+
+        @pl.when(k > 0)
+        def _():
+            main_arrival(k).wait_recv()
+
+        pass_on(k).start()
+        for side in range(2):
+            @pl.when(gets_halo[side])
+            def _():
+                halo_arrival(side, k).wait_recv()
+                halo_on(side, k).start()
+
+        passed(k).wait_recv()
+        for side in range(2):
+            @pl.when(gets_halo[side])
+            def _():
+                halo_passed(side, k).wait_recv()
+
+        def both(ref_of):
+            return jnp.concatenate([ref_of(0).astype(jnp.float32), ref_of(1).astype(jnp.float32)], axis=-1)
+
+        edges = [both(lambda h: halo[h, side, q]) for side in range(2)]
+        for x in range(wide):
+            cells = both(lambda h: recv[h, q, x])
+            for f in range(nf):
+                at = (x * nf + f) * 2
+                ext = jnp.concatenate(
+                    [edges[0][at:at + 2], cells[f * ROWS_DEV:(f + 1) * ROWS_DEV], edges[1][at:at + 2],
+                     jnp.zeros((PITCH - ROWS_DEV - 4, full), jnp.float32)], axis=0)
+                scale = lax.rsqrt(jnp.mean(ext * ext, axis=-1, keepdims=True) + norm_eps)
+                v = ext * scale * gain
+                v = v / (1.0 + jnp.exp(-v))
+                slot = q * nf + f
+                for dh in range(3):
+                    moved = v if dh == 0 else pltpu.roll(v, PITCH - dh, 0)
+                    act3[x, slot + 2, :, dh * full:(dh + 1) * full] = moved.astype(jnp.bfloat16)
+                if 0 < x < wide - 1:
+                    moved = pltpu.roll(ext, PITCH - 1, 0)
+                    own = jnp.where(c == 0, moved[:, :half], moved[:, half:])
+                    res[x - 1, slot] = own.astype(jnp.bfloat16)
+
+    for tap in taps:
+        weight_copy(*tap).wait()
+
+    def mid_copy(x):
+        return remote(mid.at[c, x + 1], mid.at[c, x + 1], m_send.at[x], m_recv.at[x], seq=s, tile=t, chan=other)
+
+    def mid_arrival(x):
+        return remote(mid.at[other, x + 1], mid.at[other, x + 1], m_send.at[x], m_recv.at[x],
+                      seq=s, tile=t, chan=other)
+
+    def edge_copy(side, far):
+        slot, landing = (1, wide - 1) if side == 0 else (wide - 2, 0)
+        return remote(mid.at[c, slot], mid.at[c, landing], e_send.at[side, far], e_recv.at[side, far],
+                      seq=s - 1 if side == 0 else s + 1, tile=t, chan=other if far else c)
+
+    def edge_arrival(side, far):
+        slot, landing = (1, wide - 1) if side == 0 else (wide - 2, 0)
+        return remote(mid.at[c, slot], mid.at[other if far else c, landing], e_send.at[side, far],
+                      e_recv.at[side, far], seq=s, tile=t, chan=other)
+
+    sends_edge = (s > 0, s < S - 1)
+    gets_edge = (s < S - 1, s > 0)
+
+    row = lax.broadcasted_iota(jnp.int32, (FRAMES, PITCH, half), 1)
+    outside = jnp.logical_or(jnp.logical_and(row == 0, t == 0),
+                             jnp.logical_and(row == ROWS_DEV + 1, t == T - 1))
+
+    @pl.loop(0, COLS_DEV)
+    def _(i):
+        x = (COLS_DEV - 1) * i % COLS_DEV
+        acc = None
+        for dt in range(3):
+            for dw in range(3):
+                lhs = act3[x + dw, dt:dt + FRAMES].reshape(FRAMES * PITCH, 3 * full)
+                part = jnp.dot(lhs, wv[dt * 3 + dw], preferred_element_type=jnp.float32)
+                acc = part if acc is None else acc + part
+        value = acc.reshape(FRAMES, PITCH, half) + cb_ref[...] + res[x].astype(jnp.float32)
+        mid[c, x + 1] = jnp.where(outside, 0.0, value).astype(jnp.bfloat16)
+        mid_copy(x).start()
+        for side, at in ((0, 0), (1, COLS_DEV - 1)):
+            @pl.when(jnp.logical_and(x == at, sends_edge[side]))
+            def _():
+                edge_copy(side, 0).start()
+                edge_copy(side, 1).start()
+
+    for x in range(COLS_DEV):
+        mid_arrival(x).wait_recv()
+    for side in range(2):
+        @pl.when(gets_edge[side])
+        def _():
+            edge_arrival(side, 0).wait_recv()
+            edge_arrival(side, 1).wait_recv()
+
+    @pl.loop(0, wide)
+    def _(x):
+        for f in range(FRAMES):
+            v = jnp.concatenate([mid[0, x, f].astype(jnp.float32), mid[1, x, f].astype(jnp.float32)], axis=-1)
+            for shift in range(3):
+                moved = v if shift == 0 else pltpu.roll(v, PITCH - shift, 0)
+                up[x, f, :, shift * full:(shift + 1) * full] = moved.astype(jnp.bfloat16)
+
+    @pl.loop(0, COLS_DEV)
+    def _(x):
+        for i in range(2):
+            acc = None
+            for b in range(3):
+                lhs = up[x + b, :, :, i * full:(i + 2) * full].reshape(FRAMES * PITCH, 2 * full)
+                part = jnp.dot(lhs, wf[i, b], preferred_element_type=jnp.float32)
+                acc = part if acc is None else acc + part
+            value = (acc + ub_ref[...]).reshape(FRAMES, PITCH, 2 * out_half)
+            out_ref[x, i] = value[:, :ROWS_DEV].astype(jnp.bfloat16)
+
+    for k in range(S):
+        if k:
+            main_copy(k).wait_send()
+        pass_on(k).wait_send()
+    for side in range(2):
+        @pl.when(sends_halo[side])
+        def _():
+            for k in range(S):
+                halo_copy(side, k).wait_send()
+
+        @pl.when(gets_halo[side])
+        def _():
+            for k in range(S):
+                halo_on(side, k).wait_send()
+
+        @pl.when(sends_edge[side])
+        def _():
+            edge_copy(side, 0).wait_send()
+            edge_copy(side, 1).wait_send()
+    for x in range(COLS_DEV):
+        mid_copy(x).wait_send()
+
+
+def fused_body(S, T, latents, norm_gain, conv_weight, conv_bias, upsample_weight, upsample_bias):
+    half = latents.shape[2]
+    full = 2 * half
+    nf = FRAMES // S
+    wide = COLS_DEV + 2
+    width = S * COLS_DEV
+    out_half = upsample_bias.shape[0]
+    cells = latents[0].reshape(nf, ROWS_DEV, width, half)
+    columns = jnp.pad(jnp.transpose(cells, (2, 0, 1, 3)), ((1, 1), (0, 0), (0, 0), (0, 0)))
+    edge_rows = -(-wide * nf * 2 // 16) * 16
+
+    def edges(rows):
+        parts = jnp.stack([rows[d * COLS_DEV:d * COLS_DEV + wide] for d in range(S)])
+        parts = parts.reshape(S, wide * nf * 2, half)
+        return jnp.pad(parts, ((0, 0), (0, edge_rows - wide * nf * 2), (0, 0)))
+
+    tops = edges(columns[:, :, ROWS_DEV - 2:])
+    bots = edges(columns[:, :, :2])
+    main = columns.reshape(width + 2, nf * ROWS_DEV, half)
+    vmem = pl.BlockSpec(memory_space=pltpu.VMEM)
+    dma = pltpu.SemaphoreType.DMA
+    bf16 = jnp.bfloat16
+    out = pl.pallas_call(
+        functools.partial(kernel, S, T),
+        out_shape=jax.ShapeDtypeStruct((COLS_DEV, 2, FRAMES, ROWS_DEV, 2 * out_half), bf16),
+        in_specs=[vmem, vmem, vmem, vmem, pl.BlockSpec(memory_space=pl.ANY), vmem, vmem, vmem],
+        out_specs=vmem,
+        scratch_shapes=[
+            pltpu.VMEM((2, S, wide, nf * ROWS_DEV, half), bf16),
+            pltpu.VMEM((2, 2, S, edge_rows, half), bf16),
+            pltpu.VMEM((wide, FRAMES + 2, PITCH, 3 * full), bf16),
+            pltpu.VMEM((COLS_DEV, FRAMES, PITCH, half), bf16),
+            pltpu.VMEM((9, 3 * full, half), bf16),
+            pltpu.VMEM((2, 3, 2 * full, 2 * out_half), bf16),
+            pltpu.VMEM((2, wide, FRAMES, PITCH, half), bf16),
+            pltpu.VMEM((wide, FRAMES, PITCH, 3 * full), bf16),
+            dma((3, 3, 3)), dma((S,)), dma((S,)), dma((S,)), dma((S,)),
+            dma((2, S)), dma((2, S)), dma((2, S)), dma((2, S)),
+            dma((COLS_DEV,)), dma((COLS_DEV,)), dma((2, 2)), dma((2, 2)),
+        ],
+        compiler_params=pltpu.CompilerParams(
+            collective_id=0, has_side_effects=True, vmem_limit_bytes=48 * 1024 * 1024
+        ),
+    )(main, tops, bots, norm_gain.reshape(1, full), conv_weight, conv_bias.reshape(1, half),
+      upsample_weight, jnp.repeat(upsample_bias, 2).reshape(1, 2 * out_half))
+    return jnp.transpose(out, (2, 3, 1, 0, 4)).reshape(FRAMES, 2 * ROWS_DEV, COLS_DEV, 2 * out_half)
+
+
 def solution(mesh):
+    S, T = mesh.shape["seq"], mesh.shape["tile"]
+    if FRAMES % S == 0 and mesh.shape["chan"] == 2:
+        body = functools.partial(fused_body, S, T)
+    else:
+        body = plain_body
     in_specs = (
         P("tile", ("groups", "seq"), "chan"),
         P(),

time: 154 us -> 59 us (0.38)
  Pallas kernels: 0 us -> 45 us
  matrix products: 37.8 us -> 0 us
  waiting for transfers between devices: 35 us -> 0 us
  blocking collectives: 28.2 us -> 0 us
  starting transfers between devices: 14.8 us -> 0 us
  between operations: 13.6 us -> 0.17 us
  local copies, waits for them, and re-layouts: 21.3 us -> 13.4 us
  other arithmetic: 3.28 us -> 0.03 us
    pallas_call x0 -> x1, Pallas kernels: none -> 45 us  [fused_body(): pl.pallas_call(functools.partial(kernel, S, T), out_shape=jax.ShapeDtypeS...]
    conv_general_dilated x2 -> x0, matrix products: 37.8 us -> none  [the longest x1 29.8 us: body(): lax.conv_general_dilated(shifted[None], conv_weight, (1, 1, 1), 'VALID',...]
    all_to_all x1 -> x0, blocking collectives: 25.4 us -> none  [body(): lax.all_to_all(arranged, 'seq', split_axis=1, concat_axis=0, tiled=True)]
    ppermute x8 -> x0, waiting for transfers between devices: 20.8 us -> none  [the longest x4 17.3 us: extended(): lax.ppermute(head, axis, [((i + 1) % count, i) for i in range(ends)])]
    ppermute x8 -> x0, starting transfers between devices: 14.8 us -> none  [the longest x4 9.67 us: extended(): lax.ppermute(tail, axis, [(i, (i + 1) % count) for i in range(ends)])]
    all_gather x1 -> x0, waiting for transfers between devices: 14.2 us -> none  [body(): middle_full = lax.all_gather(middle_rim, 'chan', axis=3, tiled=True)]
    all_gather x2 -> x0, local copies, waits for them, and re-layouts: 10.3 us -> none  [the longest x1 9.9 us: body(): middle_full = lax.all_gather(middle_rim, 'chan', axis=3, tiled=True)]
    unnamed x10 -> x8, local copies, waits for them, and re-layouts: 0.64 us -> 9.87 us
  transfers between devices with their start and end apart: 9 -> 0, of which waited for: 9 -> 0; matrix products, arithmetic and copies ran while one was open for 0% -> 0% of each run, Pallas kernels for 0% -> 0%
where the time goes in v1:
time: 59 us; the launch traced here: 58.6 us
  Pallas kernels  45 us (76%)
  local copies, waits for them, and re-layouts  13.4 us (23%)
    pallas_call x1, Pallas kernels, fused_body(): pl.pallas_call(functools.partial(kernel, S, T), out_shape=jax.ShapeDtypeS...  45 us
    unnamed x8, local copies, waits for them, and re-layouts  9.87 us

profile of v1, /device:TPU:0, one launch (start us, length us, event | category | flops | bytes accessed | tf_op | source)
XLA Modules:
  0.0 58.6 jit_solution(8938115853411554640)
XLA Ops:
  0.0 0.0 copy-start.1
  0.0 0.7 %reshape.31.gain_ref = f32[1,384]{1,0:T(1,128)S(1)} reshape(f32[384]{0:T(512)} %param.7) | data formatting | bytes 3072 | tf_op jit(solution)/shard_map/reshape | solution.py:396
  0.8 0.7 %broadcast_in_dim.3 = f32[96,2]{1,0:T(8,128)S(1)} broadcast(f32[96]{0:T(128)} %param.11), dimensions={0} | broadcast | bytes 1152 | tf_op jit(solution)/shard_map/broadcast_in_dim | solution.py:397
  1.5 0.1 reshape_reshape.3.ub_ref
  1.6 1.2 %copy.10 = bf16[1,960,192]{2,1,0:T(8,128)(2,1)S(1)} copy(bf16[1,960,192]{1,2,0:T(8,128)(2,1)} %param.6) | data formatting | bytes 737280 | tf_op args[0]
  2.8 0.1 reshape_squeeze.3
  3.2 0.1 copy.24
  3.6 0.1 pad.11.clone
  3.7 0.0 copy-done.1
  3.7 0.0 copy-start
  3.7 0.4 copy.21.uw_ref
  4.1 8.1 %copy.20.cw_ref = bf16[3,3,3,384,192]{4,3,2,1,0:T(8,128)(2,1)} copy(bf16[3,3,3,384,192]{3,4,2,1,0:T(8,128)(2,1)} %param.8) | data formatting | bytes 7962624 | tf_op args[2]
  12.2 0.0 copy-done
  12.3 45.0 %shard_map.64 = bf16[5,2,8,24,192]{4,3,2,1,0:T(8,128)(2,1)S(1)} custom-call(bf16[22,48,192]{2,1,0:T(8,128)(2,1)S(1)} %bitcast.6, bf16[4,32,192]{2,1,0:T(8,128)(2,1)S(1)} %get-tuple-element.13.tops_ref, bf16[4,32,192]{2,1,0:T(8,128)(2,1)S(1)} %get-tuple-element.14.bots_ref, f32[1,384]{1,0:T(1,128)S(1)} %reshape.31.gain_ref, ...), custom_call_target="tpu_custom_call" | custom-call | tf_op jit(solution)/shard_map/pallas_call | solution.py:375
  57.3 0.2 copy.22
  57.5 1.1 %copy.23 = bf16[8,48,5,192]{3,1,2,0:T(8,128)(2,1)} copy(bf16[8,48,5,192]{3,0,2,1:T(8,128)(2,1)S(1)} %bitcast.11) | data formatting | bytes 1474560 | tf_op jit(solution)/shard_map/reshape | solution.py:398
  (19 shorter events, 0.4 us)
Async XLA Ops:
  0.0 3.7 %copy-start.1 = (bf16[3,3,384,96]{2,3,1,0:T(8,128)(2,1)S(1)}, bf16[3,3,384,96]{2,3,1,0:T(8,128)(2,1)}, u32[]{:S(2)}) copy-start(bf16[3,3,384,96]{2,3,1,0:T(8,128)(2,1)} %param.10) | copy-start | bytes 1990660
  3.7 8.6 %copy-start = (f32[192]{0:T(256)S(1)}, f32[192]{0:T(256)}, u32[]{:S(2)}) copy-start(f32[192]{0:T(256)} %param.9) | copy-start | bytes 2308

commit v2 on v1

--- a/solution.py
+++ b/solution.py
@@ -84,19 +84,19 @@
 
 
 def kernel(S, T, main_ref, tops_ref, bots_ref, gain_ref, cw_ref, cb_ref, uw_ref, ub_ref, out_ref,
-           recv, halo, act3, res, wv, wf, mid, up,
+           recv, halo, act3, total_ref, res, wv, wf, mid, up,
            w_sem, a_send, a_recv, f_send, f_recv, h_send, h_recv, g_send, g_recv, m_send, m_recv, e_send, e_recv):
     s, t, c = lax.axis_index("seq"), lax.axis_index("tile"), lax.axis_index("chan")
     other = 1 - c
     wide = COLS_DEV + 2
     nf = FRAMES // S
-    half = main_ref.shape[2]
+    half = cb_ref.shape[1]
     full = 2 * half
 
     def weight_copy(dt, dh, dw):
         return pltpu.make_async_copy(
             cw_ref.at[dt, dh, dw],
-            wv.at[dt * 3 + dw, pl.ds(dh * full, full)],
+            wv.at[dt * 3 + dw, :, pl.ds(dh * full, full)],
             w_sem.at[dt, dh, dw],
         )
 
@@ -184,11 +184,11 @@
     def _():
         mid[:, wide - 1] = jnp.zeros(mid.shape[:1] + mid.shape[2:], mid.dtype)
 
-    act3[:, 0:2] = jnp.zeros((wide, 2) + act3.shape[2:], act3.dtype)
-
-    out_half = uw_ref.shape[3]
-    source = lax.broadcasted_iota(jnp.int32, (out_half, 2 * out_half), 0)
-    target = lax.broadcasted_iota(jnp.int32, (out_half, 2 * out_half), 1)
+    total_ref[...] = jnp.zeros(total_ref.shape, total_ref.dtype)
+
+    out_half = uw_ref.shape[2]
+    source = lax.broadcasted_iota(jnp.int32, (2 * out_half, out_half), 1)
+    target = lax.broadcasted_iota(jnp.int32, (2 * out_half, out_half), 0)
     spread = [jnp.where(target == 2 * source + j, 1.0, 0.0).astype(jnp.bfloat16) for j in range(2)]
     row_taps = (((0,), (1, 2)), ((0, 1), (2,)))
     col_taps = (((0,), ()), ((1, 2), (0, 1)), ((), (2,)))
@@ -201,11 +201,17 @@
                         continue
                     terms = [uw_ref[dr, dc].astype(jnp.float32) for dr in row_taps[i][a] for dc in col_taps[b][j]]
                     value = functools.reduce(lambda u, v: u + v, terms).astype(jnp.bfloat16)
-                    part = jnp.dot(value, spread[j], preferred_element_type=jnp.float32)
+                    part = jnp.dot(spread[j], value, preferred_element_type=jnp.float32)
                     total = part if total is None else total + part
-                wf[i, b, a * full:(a + 1) * full] = total.astype(jnp.bfloat16)
+                wf[i, b, :, a * full:(a + 1) * full] = total.astype(jnp.bfloat16)
 
     gain = gain_ref[...]
+
+    def dot(lhs, rhs):
+        return lax.dot_general(lhs, rhs, (((1,), (1,)), ((), ())), preferred_element_type=jnp.float32)
+
+    for tap in taps:
+        weight_copy(*tap).wait()
 
     @pl.loop(0, S)
     def _(k):
@@ -233,15 +239,16 @@
                 halo_passed(side, k).wait_recv()
 
         def both(ref_of):
-            return jnp.concatenate([ref_of(0).astype(jnp.float32), ref_of(1).astype(jnp.float32)], axis=-1)
+            parts = [ref_of(h).astype(jnp.float32) for h in range(2)]
+            return [jnp.concatenate([p[:, f * half:(f + 1) * half] for p in parts], axis=-1) for f in range(nf)]
 
         edges = [both(lambda h: halo[h, side, q]) for side in range(2)]
         for x in range(wide):
             cells = both(lambda h: recv[h, q, x])
             for f in range(nf):
-                at = (x * nf + f) * 2
+                at = x * 2
                 ext = jnp.concatenate(
-                    [edges[0][at:at + 2], cells[f * ROWS_DEV:(f + 1) * ROWS_DEV], edges[1][at:at + 2],
+                    [edges[0][f][at:at + 2], cells[f], edges[1][f][at:at + 2],
                      jnp.zeros((PITCH - ROWS_DEV - 4, full), jnp.float32)], axis=0)
                 scale = lax.rsqrt(jnp.mean(ext * ext, axis=-1, keepdims=True) + norm_eps)
                 v = ext * scale * gain
@@ -249,14 +256,19 @@
                 slot = q * nf + f
                 for dh in range(3):
                     moved = v if dh == 0 else pltpu.roll(v, PITCH - dh, 0)
-                    act3[x, slot + 2, :, dh * full:(dh + 1) * full] = moved.astype(jnp.bfloat16)
+                    act3[x, f, :, dh * full:(dh + 1) * full] = moved.astype(jnp.bfloat16)
                 if 0 < x < wide - 1:
                     moved = pltpu.roll(ext, PITCH - 1, 0)
                     own = jnp.where(c == 0, moved[:, :half], moved[:, half:])
                     res[x - 1, slot] = own.astype(jnp.bfloat16)
 
-    for tap in taps:
-        weight_copy(*tap).wait()
+        for dt in range(3):
+            acc = None
+            for dw in range(3):
+                lhs = act3[dw:dw + COLS_DEV].reshape(COLS_DEV * nf * PITCH, 3 * full)
+                part = dot(lhs, wv[dt * 3 + dw])
+                acc = part if acc is None else acc + part
+            total_ref[:, pl.ds(q * nf + 2 - dt, nf)] += acc.reshape(COLS_DEV, nf, PITCH, half)
 
     def mid_copy(x):
         return remote(mid.at[c, x + 1], mid.at[c, x + 1], m_send.at[x], m_recv.at[x], seq=s, tile=t, chan=other)
@@ -265,15 +277,20 @@
         return remote(mid.at[other, x + 1], mid.at[other, x + 1], m_send.at[x], m_recv.at[x],
                       seq=s, tile=t, chan=other)
 
-    def edge_copy(side, far):
+    def edge_copy(side):
         slot, landing = (1, wide - 1) if side == 0 else (wide - 2, 0)
-        return remote(mid.at[c, slot], mid.at[c, landing], e_send.at[side, far], e_recv.at[side, far],
-                      seq=s - 1 if side == 0 else s + 1, tile=t, chan=other if far else c)
-
-    def edge_arrival(side, far):
-        slot, landing = (1, wide - 1) if side == 0 else (wide - 2, 0)
-        return remote(mid.at[c, slot], mid.at[other if far else c, landing], e_send.at[side, far],
-                      e_recv.at[side, far], seq=s, tile=t, chan=other)
+        return remote(mid.at[c, slot], mid.at[c, landing], e_send.at[side, 0], e_recv.at[side, 0],
+                      seq=s - 1 if side == 0 else s + 1, tile=t, chan=c)
+
+    def edge_on(side):
+        landing = wide - 1 if side == 0 else 0
+        return remote(mid.at[c, landing], mid.at[c, landing], e_send.at[side, 1], e_recv.at[side, 1],
+                      seq=s, tile=t, chan=other)
+
+    def edge_passed(side):
+        landing = wide - 1 if side == 0 else 0
+        return remote(mid.at[other, landing], mid.at[other, landing], e_send.at[side, 1], e_recv.at[side, 1],
+                      seq=s, tile=t, chan=other)
 
     sends_edge = (s > 0, s < S - 1)
     gets_edge = (s < S - 1, s > 0)
@@ -285,47 +302,60 @@
     @pl.loop(0, COLS_DEV)
     def _(i):
         x = (COLS_DEV - 1) * i % COLS_DEV
-        acc = None
-        for dt in range(3):
-            for dw in range(3):
-                lhs = act3[x + dw, dt:dt + FRAMES].reshape(FRAMES * PITCH, 3 * full)
-                part = jnp.dot(lhs, wv[dt * 3 + dw], preferred_element_type=jnp.float32)
-                acc = part if acc is None else acc + part
-        value = acc.reshape(FRAMES, PITCH, half) + cb_ref[...] + res[x].astype(jnp.float32)
+        value = total_ref[x, 0:FRAMES] + cb_ref[...] + res[x].astype(jnp.float32)
         mid[c, x + 1] = jnp.where(outside, 0.0, value).astype(jnp.bfloat16)
-        mid_copy(x).start()
         for side, at in ((0, 0), (1, COLS_DEV - 1)):
             @pl.when(jnp.logical_and(x == at, sends_edge[side]))
             def _():
-                edge_copy(side, 0).start()
-                edge_copy(side, 1).start()
+                edge_copy(side).start()
+        mid_copy(x).start()
 
     for x in range(COLS_DEV):
         mid_arrival(x).wait_recv()
-    for side in range(2):
-        @pl.when(gets_edge[side])
-        def _():
-            edge_arrival(side, 0).wait_recv()
-            edge_arrival(side, 1).wait_recv()
-
-    @pl.loop(0, wide)
-    def _(x):
+
+    def lay(x):
         for f in range(FRAMES):
             v = jnp.concatenate([mid[0, x, f].astype(jnp.float32), mid[1, x, f].astype(jnp.float32)], axis=-1)
             for shift in range(3):
                 moved = v if shift == 0 else pltpu.roll(v, PITCH - shift, 0)
                 up[x, f, :, shift * full:(shift + 1) * full] = moved.astype(jnp.bfloat16)
 
-    @pl.loop(0, COLS_DEV)
-    def _(x):
+    def emit(x):
         for i in range(2):
             acc = None
             for b in range(3):
                 lhs = up[x + b, :, :, i * full:(i + 2) * full].reshape(FRAMES * PITCH, 2 * full)
-                part = jnp.dot(lhs, wf[i, b], preferred_element_type=jnp.float32)
+                part = dot(lhs, wf[i, b])
                 acc = part if acc is None else acc + part
             value = (acc + ub_ref[...]).reshape(FRAMES, PITCH, 2 * out_half)
             out_ref[x, i] = value[:, :ROWS_DEV].astype(jnp.bfloat16)
+
+    @pl.loop(1, wide - 1)
+    def _(x):
+        lay(x)
+
+    for side in range(2):
+        @pl.when(gets_edge[side])
+        def _():
+            edge_copy(side).wait_recv()
+            edge_on(side).start()
+
+    @pl.loop(1, COLS_DEV - 1)
+    def _(x):
+        emit(x)
+
+    for side in range(2):
+        @pl.when(gets_edge[side])
+        def _():
+            edge_passed(side).wait_recv()
+
+    @pl.loop(0, 2)
+    def _(i):
+        lay(i * (wide - 1))
+
+    @pl.loop(0, 2)
+    def _(i):
+        emit(i * (COLS_DEV - 1))
 
     for k in range(S):
         if k:
@@ -344,8 +374,11 @@
 
         @pl.when(sends_edge[side])
         def _():
-            edge_copy(side, 0).wait_send()
-            edge_copy(side, 1).wait_send()
+            edge_copy(side).wait_send()
+
+        @pl.when(gets_edge[side])
+        def _():
+            edge_on(side).wait_send()
     for x in range(COLS_DEV):
         mid_copy(x).wait_send()
 
@@ -358,32 +391,33 @@
     width = S * COLS_DEV
     out_half = upsample_bias.shape[0]
     cells = latents[0].reshape(nf, ROWS_DEV, width, half)
-    columns = jnp.pad(jnp.transpose(cells, (2, 0, 1, 3)), ((1, 1), (0, 0), (0, 0), (0, 0)))
-    edge_rows = -(-wide * nf * 2 // 16) * 16
+    main = jnp.transpose(cells, (2, 1, 0, 3)).reshape(width, ROWS_DEV, nf * half)
+    main = jnp.pad(main, ((1, 1), (0, 0), (0, 0)))
+    edge_rows = -(-wide * 2 // 16) * 16
 
     def edges(rows):
         parts = jnp.stack([rows[d * COLS_DEV:d * COLS_DEV + wide] for d in range(S)])
-        parts = parts.reshape(S, wide * nf * 2, half)
-        return jnp.pad(parts, ((0, 0), (0, edge_rows - wide * nf * 2), (0, 0)))
-
-    tops = edges(columns[:, :, ROWS_DEV - 2:])
-    bots = edges(columns[:, :, :2])
-    main = columns.reshape(width + 2, nf * ROWS_DEV, half)
+        parts = parts.reshape(S, wide * 2, nf * half)
+        return jnp.pad(parts, ((0, 0), (0, edge_rows - wide * 2), (0, 0)))
+
+    tops = edges(main[:, ROWS_DEV - 2:])
+    bots = edges(main[:, :2])
     vmem = pl.BlockSpec(memory_space=pltpu.VMEM)
     dma = pltpu.SemaphoreType.DMA
     bf16 = jnp.bfloat16
     out = pl.pallas_call(
         functools.partial(kernel, S, T),
         out_shape=jax.ShapeDtypeStruct((COLS_DEV, 2, FRAMES, ROWS_DEV, 2 * out_half), bf16),
-        in_specs=[vmem, vmem, vmem, vmem, pl.BlockSpec(memory_space=pl.ANY), vmem, vmem, vmem],
+        in_specs=[vmem, vmem, vmem, vmem, pl.BlockSpec(memory_space=pltpu.HBM), vmem, vmem, vmem],
         out_specs=vmem,
         scratch_shapes=[
-            pltpu.VMEM((2, S, wide, nf * ROWS_DEV, half), bf16),
-            pltpu.VMEM((2, 2, S, edge_rows, half), bf16),
-            pltpu.VMEM((wide, FRAMES + 2, PITCH, 3 * full), bf16),
+            pltpu.VMEM((2, S, wide, ROWS_DEV, nf * half), bf16),
+            pltpu.VMEM((2, 2, S, edge_rows, nf * half), bf16),
+            pltpu.VMEM((wide, nf, PITCH, 3 * full), bf16),
+            pltpu.VMEM((COLS_DEV, FRAMES + 2, PITCH, half), jnp.float32),
             pltpu.VMEM((COLS_DEV, FRAMES, PITCH, half), bf16),
-            pltpu.VMEM((9, 3 * full, half), bf16),
-            pltpu.VMEM((2, 3, 2 * full, 2 * out_half), bf16),
+            pltpu.VMEM((9, half, 3 * full), bf16),
+            pltpu.VMEM((2, 3, 2 * out_half, 2 * full), bf16),
             pltpu.VMEM((2, wide, FRAMES, PITCH, half), bf16),
             pltpu.VMEM((wide, FRAMES, PITCH, 3 * full), bf16),
             dma((3, 3, 3)), dma((S,)), dma((S,)), dma((S,)), dma((S,)),
@@ -393,8 +427,8 @@
         compiler_params=pltpu.CompilerParams(
             collective_id=0, has_side_effects=True, vmem_limit_bytes=48 * 1024 * 1024
         ),
-    )(main, tops, bots, norm_gain.reshape(1, full), conv_weight, conv_bias.reshape(1, half),
-      upsample_weight, jnp.repeat(upsample_bias, 2).reshape(1, 2 * out_half))
+    )(main, tops, bots, norm_gain.reshape(1, full), jnp.transpose(conv_weight, (0, 1, 2, 4, 3)),
+      conv_bias.reshape(1, half), jnp.transpose(upsample_weight, (0, 1, 3, 2)), jnp.repeat(upsample_bias, 2).reshape(1, 2 * out_half))
     return jnp.transpose(out, (2, 3, 1, 0, 4)).reshape(FRAMES, 2 * ROWS_DEV, COLS_DEV, 2 * out_half)
 
 

time: 59 us -> 48.7 us (0.83)
  local copies, waits for them, and re-layouts: 13.4 us -> 7.5 us
  Pallas kernels: 45 us -> 40.9 us
    unnamed x8 -> x7, local copies, waits for them, and re-layouts: 9.87 us -> 3.33 us
    pallas_call x1, Pallas kernels: 45 us -> 40.9 us  [fused_body(): pl.pallas_call(functools.partial(kernel, S, T), out_shape=jax.ShapeDtypeS...]
where the time goes in v2:
time: 48.7 us; the launch traced here: 48.5 us
  Pallas kernels  40.9 us (84%)
  local copies, waits for them, and re-layouts  7.5 us (15%)
    pallas_call x1, Pallas kernels, fused_body(): pl.pallas_call(functools.partial(kernel, S, T), out_shape=jax.ShapeDtypeS...  40.9 us
    unnamed x7, local copies, waits for them, and re-layouts  3.33 us
    reshape x1, local copies, waits for them, and re-layouts, fused_body(): jnp.transpose(out, (2, 3, 1, 0, 4))  1.14 us

profile of v2, /device:TPU:0, one launch (start us, length us, event | category | flops | bytes accessed | tf_op | source)
XLA Modules:
  0.0 48.5 jit_solution(1568507782329414180)
XLA Ops:
  0.0 0.0 copy-start.1
  0.0 0.0 copy-start.2
  0.0 0.7 %reshape.31.gain_ref = f32[1,384]{1,0:T(1,128)S(1)} reshape(f32[384]{0:T(512)} %param.7) | data formatting | bytes 3072 | tf_op jit(solution)/shard_map/reshape | solution.py:430
  0.8 0.7 %broadcast_in_dim.3 = f32[96,2]{1,0:T(8,128)S(1)} broadcast(f32[96]{0:T(128)} %param.11), dimensions={0} | broadcast | bytes 1152 | tf_op jit(solution)/shard_map/broadcast_in_dim | solution.py:431
  1.5 0.1 reshape_reshape.3.ub_ref
  1.6 1.2 %copy.8 = bf16[1,960,192]{2,1,0:T(8,128)(2,1)S(1)} copy(bf16[1,960,192]{1,2,0:T(8,128)(2,1)} %param.6) | data formatting | bytes 737280 | tf_op args[0]
  2.8 0.1 reshape_squeeze.3
  3.0 0.5 %copy.9 = bf16[20,24,2,192]{3,2,1,0:T(2,128)(2,1)S(1)} copy(bf16[20,24,2,192]{3,0,1,2:T(8,128)(2,1)S(1)} %bitcast.11) | data formatting | bytes 737280 | tf_op jit(solution)/shard_map/transpose | solution.py:394
  3.5 0.2 reshape.30
  4.1 0.0 copy-done.1
  4.1 0.0 copy-done.2
  4.1 0.0 copy-start
  4.2 2.1 %copy-done = bf16[3,3,3,384,192]{3,4,2,1,0:T(8,128)(2,1)S(1)} copy-done((bf16[3,3,3,384,192]{3,4,2,1,0:T(8,128)(2,1)S(1)}, bf16[3,3,3,384,192]{3,4,2,1,0:T(8,128)(2,1)}, u32[]{:S(2)}) %copy-start) | copy-done | bytes 3981336
  6.3 40.9 %shard_map.64 = bf16[5,2,8,24,192]{4,3,2,1,0:T(8,128)(2,1)S(1)} custom-call(bf16[22,24,384]{2,1,0:T(8,128)(2,1)S(1)} %pad.11.main_ref, bf16[4,16,384]{2,1,0:T(8,128)(2,1)S(1)} %get-tuple-element.13.tops_ref, bf16[4,16,384]{2,1,0:T(8,128)(2,1)S(1)} %get-tuple-element.14.bots_ref, f32[1,384]{1,0:T(1,128)S(1)} %reshape.31.gain_ref, ...), custom_call_target="tpu_custom_call" | custom-call | tf_op jit(solution)/shard_map/pallas_call | solution.py:408
  47.2 0.2 copy.10
  47.4 1.1 %copy.11 = bf16[8,48,5,192]{3,1,2,0:T(8,128)(2,1)} copy(bf16[8,48,5,192]{3,0,2,1:T(8,128)(2,1)S(1)} %bitcast.10) | data formatting | bytes 1474560 | tf_op jit(solution)/shard_map/reshape | solution.py:432
  (12 shorter events, 0.4 us)
Async XLA Ops:
  0.0 4.1 %copy-start.1 = (bf16[3,3,384,96]{2,3,1,0:T(8,128)(2,1)S(1)}, bf16[3,3,384,96]{2,3,1,0:T(8,128)(2,1)}, u32[]{:S(2)}) copy-start(bf16[3,3,384,96]{2,3,1,0:T(8,128)(2,1)} %param.10) | copy-start | bytes 1990660
  0.0 4.1 %copy-start.2 = (f32[192]{0:T(256)S(1)}, f32[192]{0:T(256)}, u32[]{:S(2)}) copy-start(f32[192]{0:T(256)} %param.9) | copy-start | bytes 2308
  4.1 2.1 %copy-start = (bf16[3,3,3,384,192]{3,4,2,1,0:T(8,128)(2,1)S(1)}, bf16[3,3,3,384,192]{3,4,2,1,0:T(8,128)(2,1)}, u32[]{:S(2)}) copy-start(bf16[3,3,3,384,192]{3,4,2,1,0:T(8,128)(2,1)} %param.8) | copy-start | bytes 11943940

commit v3 on v2

--- a/solution.py
+++ b/solution.py
@@ -84,7 +84,7 @@
 
 
 def kernel(S, T, main_ref, tops_ref, bots_ref, gain_ref, cw_ref, cb_ref, uw_ref, ub_ref, out_ref,
-           recv, halo, act3, total_ref, res, wv, wf, mid, up,
+           recv, halo, act3, total_ref, res, wv, wf, mid, up, image_bias,
            w_sem, a_send, a_recv, f_send, f_recv, h_send, h_recv, g_send, g_recv, m_send, m_recv, e_send, e_recv):
     s, t, c = lax.axis_index("seq"), lax.axis_index("tile"), lax.axis_index("chan")
     other = 1 - c
@@ -120,43 +120,47 @@
             src_ref=src, dst_ref=dst, send_sem=send, recv_sem=recv_, device_id=where, device_id_type=MESH
         )
 
+    def partner(k):
+        bits = [b for b in range(S.bit_length() - 1)]
+        return sum(((s // 2**b + k // 2**b) % 2 * 2**b for b in bits), 0 * s)
+
     def main_copy(k):
-        d = (s + S - k) % S
+        d = partner(k)
         return remote(main_ref.at[pl.ds(d * COLS_DEV, wide)], recv.at[c, s], a_send.at[k], a_recv.at[k],
                       seq=d, tile=t, chan=c)
 
     def main_arrival(k):
-        q = (s + k) % S
+        q = partner(k)
         return remote(main_ref.at[pl.ds(0, wide)], recv.at[c, q], a_send.at[k], a_recv.at[k], seq=q, tile=t, chan=c)
 
     own_copy = pltpu.make_async_copy(main_ref.at[pl.ds(s * COLS_DEV, wide)], recv.at[c, s], a_recv.at[0])
 
     def pass_on(k):
-        q = (s + k) % S
+        q = partner(k)
         return remote(recv.at[c, q], recv.at[c, q], f_send.at[k], f_recv.at[k], seq=s, tile=t, chan=other)
 
     def passed(k):
-        q = (s + k) % S
+        q = partner(k)
         return remote(recv.at[other, q], recv.at[other, q], f_send.at[k], f_recv.at[k], seq=s, tile=t, chan=other)
 
     def halo_copy(side, k):
-        d = (s + S - k) % S
+        d = partner(k)
         src = tops_ref if side == 0 else bots_ref
         to = t + 1 if side == 0 else t - 1
         return remote(src.at[d], halo.at[c, side, s], h_send.at[side, k], h_recv.at[side, k], seq=d, tile=to, chan=c)
 
     def halo_arrival(side, k):
-        q = (s + k) % S
+        q = partner(k)
         return remote(tops_ref.at[0], halo.at[c, side, q], h_send.at[side, k], h_recv.at[side, k],
                       seq=q, tile=t, chan=other)
 
     def halo_on(side, k):
-        q = (s + k) % S
+        q = partner(k)
         return remote(halo.at[c, side, q], halo.at[c, side, q], g_send.at[side, k], g_recv.at[side, k],
                       seq=s, tile=t, chan=other)
 
     def halo_passed(side, k):
-        q = (s + k) % S
+        q = partner(k)
         return remote(halo.at[other, side, q], halo.at[other, side, q], g_send.at[side, k], g_recv.at[side, k],
                       seq=s, tile=t, chan=other)
 
@@ -164,7 +168,7 @@
     gets_halo = (t > 0, t < T - 1)
 
     own_copy.start()
-    for k in range(S - 1, 0, -1):
+    for k in range(1, S):
         main_copy(k).start()
     for side in range(2):
         @pl.when(sends_halo[side])
@@ -205,6 +209,11 @@
                     total = part if total is None else total + part
                 wf[i, b, :, a * full:(a + 1) * full] = total.astype(jnp.bfloat16)
 
+    both_bias = sum(
+        lax.dot_general(jnp.broadcast_to(ub_ref[...], (8, out_half)), m.astype(jnp.float32), (((1,), (1,)), ((), ())),
+                        precision=lax.Precision.HIGHEST, preferred_element_type=jnp.float32)
+        for m in spread)
+    image_bias[...] = both_bias[:1]
     gain = gain_ref[...]
 
     def dot(lhs, rhs):
@@ -215,7 +224,7 @@
 
     @pl.loop(0, S)
     def _(k):
-        q = (s + k) % S
+        q = partner(k)
 
         @pl.when(k == 0)
         def _():
@@ -252,7 +261,7 @@
                      jnp.zeros((PITCH - ROWS_DEV - 4, full), jnp.float32)], axis=0)
                 scale = lax.rsqrt(jnp.mean(ext * ext, axis=-1, keepdims=True) + norm_eps)
                 v = ext * scale * gain
-                v = v / (1.0 + jnp.exp(-v))
+                v = 0.5 * v * (1.0 + jnp.tanh(0.5 * v))
                 slot = q * nf + f
                 for dh in range(3):
                     moved = v if dh == 0 else pltpu.roll(v, PITCH - dh, 0)
@@ -327,7 +336,7 @@
                 lhs = up[x + b, :, :, i * full:(i + 2) * full].reshape(FRAMES * PITCH, 2 * full)
                 part = dot(lhs, wf[i, b])
                 acc = part if acc is None else acc + part
-            value = (acc + ub_ref[...]).reshape(FRAMES, PITCH, 2 * out_half)
+            value = (acc + image_bias[...]).reshape(FRAMES, PITCH, 2 * out_half)
             out_ref[x, i] = value[:, :ROWS_DEV].astype(jnp.bfloat16)
 
     @pl.loop(1, wide - 1)
@@ -420,15 +429,16 @@
             pltpu.VMEM((2, 3, 2 * out_half, 2 * full), bf16),
             pltpu.VMEM((2, wide, FRAMES, PITCH, half), bf16),
             pltpu.VMEM((wide, FRAMES, PITCH, 3 * full), bf16),
+            pltpu.VMEM((1, 2 * out_half), jnp.float32),
             dma((3, 3, 3)), dma((S,)), dma((S,)), dma((S,)), dma((S,)),
             dma((2, S)), dma((2, S)), dma((2, S)), dma((2, S)),
             dma((COLS_DEV,)), dma((COLS_DEV,)), dma((2, 2)), dma((2, 2)),
         ],
         compiler_params=pltpu.CompilerParams(
-            collective_id=0, has_side_effects=True, vmem_limit_bytes=48 * 1024 * 1024
+            collective_id=0, has_side_effects=True, vmem_limit_bytes=50 * 1024 * 1024
         ),
     )(main, tops, bots, norm_gain.reshape(1, full), jnp.transpose(conv_weight, (0, 1, 2, 4, 3)),
-      conv_bias.reshape(1, half), jnp.transpose(upsample_weight, (0, 1, 3, 2)), jnp.repeat(upsample_bias, 2).reshape(1, 2 * out_half))
+      conv_bias.reshape(1, half), jnp.transpose(upsample_weight, (0, 1, 3, 2)), upsample_bias.reshape(1, out_half))
     return jnp.transpose(out, (2, 3, 1, 0, 4)).reshape(FRAMES, 2 * ROWS_DEV, COLS_DEV, 2 * out_half)
 
 

time: 48.7 us -> 42.1 us (0.86)
  Pallas kernels: 40.9 us -> 37.3 us
  local copies, waits for them, and re-layouts: 7.5 us -> 4.51 us
    pallas_call x1, Pallas kernels: 40.9 us -> 37.3 us  [fused_body(): pl.pallas_call(functools.partial(kernel, S, T), out_shape=jax.ShapeDtypeS...]
    unnamed x7, local copies, waits for them, and re-layouts: 3.33 us -> 1.21 us
    broadcast_in_dim x1 -> x0, local copies, waits for them, and re-layouts: 0.73 us -> none  [fused_body(): jnp.repeat(upsample_bias, 2).reshape(1, 2 * out_half)]
where the time goes in v3:
time: 42.1 us; the launch traced here: 41.9 us
  Pallas kernels  37.3 us (89%)
  local copies, waits for them, and re-layouts  4.51 us (11%)
    pallas_call x1, Pallas kernels, fused_body(): pl.pallas_call(functools.partial(kernel, S, T), out_shape=jax.ShapeDtypeS...  37.3 us
    unnamed x7, local copies, waits for them, and re-layouts  1.21 us
    reshape x1, local copies, waits for them, and re-layouts, fused_body(): jnp.transpose(out, (2, 3, 1, 0, 4))  1.14 us

profile of v3, /device:TPU:0, one launch (start us, length us, event | category | flops | bytes accessed | tf_op | source)
XLA Modules:
  0.0 41.9 jit_solution(11304491842574240597)
XLA Ops:
  0.0 0.0 copy-start.2
  0.0 0.0 copy-start
  0.0 0.0 copy-start.1
  0.0 0.7 %reshape.34.gain_ref = f32[1,384]{1,0:T(1,128)S(1)} reshape(f32[384]{0:T(512)} %param.7) | data formatting | bytes 3072 | tf_op jit(solution)/shard_map/reshape | solution.py:440
  0.8 1.2 %copy.8 = bf16[1,960,192]{2,1,0:T(8,128)(2,1)S(1)} copy(bf16[1,960,192]{1,2,0:T(8,128)(2,1)} %param.6) | data formatting | bytes 737280 | tf_op args[0]
  2.0 0.1 reshape_squeeze.3
  2.1 0.5 %copy.9 = bf16[20,24,2,192]{3,2,1,0:T(2,128)(2,1)S(1)} copy(bf16[20,24,2,192]{3,0,1,2:T(8,128)(2,1)S(1)} %bitcast.13) | data formatting | bytes 737280 | tf_op jit(solution)/shard_map/transpose | solution.py:403
  2.6 0.2 reshape.33
  3.3 0.0 copy-done.2
  3.3 0.0 copy-done
  3.3 0.0 copy-done.1
  3.3 37.3 %shard_map.64 = bf16[5,2,8,24,192]{4,3,2,1,0:T(8,128)(2,1)S(1)} custom-call(bf16[22,24,384]{2,1,0:T(8,128)(2,1)S(1)} %pad.11.main_ref, bf16[4,16,384]{2,1,0:T(8,128)(2,1)S(1)} %get-tuple-element.13.tops_ref, bf16[4,16,384]{2,1,0:T(8,128)(2,1)S(1)} %get-tuple-element.14.bots_ref, f32[1,384]{1,0:T(1,128)S(1)} %reshape.34.gain_ref, ...), custom_call_target="tpu_custom_call" | custom-call | tf_op jit(solution)/shard_map/pallas_call | solution.py:417
  40.6 0.2 copy.10
  40.8 1.1 %copy.11 = bf16[8,48,5,192]{3,1,2,0:T(8,128)(2,1)} copy(bf16[8,48,5,192]{3,0,2,1:T(8,128)(2,1)S(1)} %bitcast.12) | data formatting | bytes 1474560 | tf_op jit(solution)/shard_map/reshape | solution.py:442
  (12 shorter events, 0.4 us)
Async XLA Ops:
  0.0 3.3 %copy-start.2 = (f32[96]{0:T(128)S(1)}, f32[96]{0:T(128)}, u32[]{:S(2)}) copy-start(f32[96]{0:T(128)} %param.11) | copy-start | bytes 1156
  0.0 3.3 %copy-start = (bf16[3,3,384,96]{2,3,1,0:T(8,128)(2,1)S(1)}, bf16[3,3,384,96]{2,3,1,0:T(8,128)(2,1)}, u32[]{:S(2)}) copy-start(bf16[3,3,384,96]{2,3,1,0:T(8,128)(2,1)} %param.10) | copy-start | bytes 1990660
  0.0 3.3 %copy-start.1 = (f32[192]{0:T(256)S(1)}, f32[192]{0:T(256)}, u32[]{:S(2)}) copy-start(f32[192]{0:T(256)} %param.9) | copy-start | bytes 2308
